TPU v7x, 256 devices: a whole 4x4x8 slice. The times are simulated.
256 devices in a mesh: batch: 16 (over z_hi, x), seq: 16 (over z_lo, y, core).
Axes of the slice: x: 4, y: 4, z: 8 (z_hi: 4, z_lo: 2; z = z_hi * 2 + z_lo), core: 2. Of those that a mesh axis runs over, the one named last changes fastest.
Arguments:
- tower_input: bfloat16 [16, 2048, 1536], P('batch', 'seq'), may hold values from -36 to 36
- norm_gain: float32 [1536], replicated, may hold values from 0.1 to 1.9
- conv_weight: bfloat16 [3, 1536, 768], P(None, 'seq', 'batch'), may hold values from -0.09375 to 0.09375
- mix_weight: bfloat16 [768, 1536], P('batch', 'seq'), may hold values from -0.21875 to 0.21875
- head_weight: bfloat16 [1536, 4096], P(None, 'seq'), may hold values from -0.15625 to 0.15625
- head_bias: float32 [4096], replicated, may hold values from -2 to 1
- pred_cotangent: bfloat16 [16, 2048, 4096], P('batch', 'seq'), may hold values from -6 to 6
Outputs:
- predictions: bfloat16 [16, 2048, 4096], P('batch', 'seq')
- input_grad: bfloat16 [16, 2048, 1536], P('batch', 'seq')
- conv_grad: float32 [3, 1536, 768], P(None, 'seq', 'batch')
- mix_grad: float32 [768, 1536], P('batch', 'seq')
All inputs are finite; a program needn't handle non-finite values.
Results may differ from a plain program's by a relative error of at most 0.035.
Values may be sent and summed in bfloat16 or wider, within the bound.
A program may use at most 128 MiB of HBM per device.

v0:
```python
import jax
import jax.numpy as jnp
from jax import lax
from jax.sharding import PartitionSpec as P

CH = 1536
INNER = 768
DILATION_STEP = 8


def extended(cells, sides, width):
    for axis, dim in sides:
        count = lax.axis_size(axis)
        ends = count - 1
        head = lax.slice_in_dim(cells, 0, width, axis=dim)
        tail = lax.slice_in_dim(cells, cells.shape[dim] - width, cells.shape[dim], axis=dim)
        cells = jnp.concatenate(
            [
                lax.ppermute(tail, axis, [(i, (i + 1) % count) for i in range(ends)]),
                cells,
                lax.ppermute(head, axis, [((i + 1) % count, i) for i in range(ends)]),
            ],
            axis=dim,
        )
    return cells


def gelu_tanh(values):
    return jax.nn.gelu(values, approximate=True)


def activate(inputs, norm_gain):
    mean_sq = jnp.mean(inputs * inputs, axis=-1, keepdims=True)
    return gelu_tanh(inputs * lax.rsqrt(mean_sq + 1e-06) * norm_gain)


def body(tower_input, norm_gain, conv_weight, mix_weight, head_weight, head_bias, pred_cotangent):
    contract_last = (((1,), (1,)), ((), ()))
    contract_first = (((0,), (0,)), ((), ()))
    conv_part_w, mix_part_w = (
        lax.all_gather(conv_weight, "batch", axis=2, tiled=True),
        lax.all_gather(mix_weight, "batch", axis=0, tiled=True),
    )
    conv_weight, mix_weight = (
        lax.all_gather(conv_part_w, "seq", axis=1, tiled=True),
        lax.all_gather(mix_part_w, "seq", axis=1, tiled=True),
    )
    inputs = tower_input[0].astype(jnp.float32)
    total_row_count = inputs.shape[0]
    gelu_output = activate(inputs, norm_gain).astype(jnp.bfloat16)
    padded_input = extended(gelu_output, (("seq", 0),), DILATION_STEP)
    kernel_tap_rows = [
        padded_input[
            kernel_tap_index * DILATION_STEP : kernel_tap_index * DILATION_STEP + total_row_count
        ]
        for kernel_tap_index in range(3)
    ]
    conv_out = jnp.zeros((total_row_count, INNER), jnp.float32)
    for kernel_tap_index in range(3):
        conv_out = conv_out + jnp.dot(
            kernel_tap_rows[kernel_tap_index],
            conv_weight[kernel_tap_index],
            preferred_element_type=jnp.float32,
        )
    hidden = gelu_tanh(conv_out).astype(jnp.bfloat16)
    tower_out = (inputs + jnp.dot(hidden, mix_weight, preferred_element_type=jnp.float32)).astype(
        jnp.bfloat16
    )
    groups = lax.axis_size("seq")
    width_dev = head_weight.shape[1]
    bias_part = lax.dynamic_slice_in_dim(head_bias, lax.axis_index("seq") * width_dev, width_dev)
    logits = (
        jnp.dot(
            lax.all_gather(tower_out, "seq", axis=0, tiled=True),
            head_weight,
            preferred_element_type=jnp.float32,
        )
        + bias_part
    )
    pred_local = jax.nn.softplus(logits).astype(jnp.bfloat16)
    predictions = lax.all_to_all(pred_local, "seq", split_axis=0, concat_axis=1, tiled=True)
    cot_local = lax.all_to_all(pred_cotangent[0], "seq", split_axis=1, concat_axis=0, tiled=True)
    dlogits = (cot_local.astype(jnp.float32) * jax.nn.sigmoid(logits)).astype(jnp.bfloat16)
    dtower = lax.psum_scatter(
        lax.dot_general(
            dlogits, head_weight, contract_last, preferred_element_type=jnp.float32
        ).astype(jnp.bfloat16),
        "seq",
        scatter_dimension=0,
        tiled=True,
    ).astype(jnp.float32)
    dtower_half = dtower.astype(jnp.bfloat16)
    dhidden = lax.dot_general(
        dtower_half, mix_weight, contract_last, preferred_element_type=jnp.float32
    )
    conv_output_gradient = jax.vjp(gelu_tanh, conv_out)[1](dhidden)[0].astype(jnp.bfloat16)
    padded_input_gradient = extended(conv_output_gradient, (("seq", 0),), DILATION_STEP)
    dactivated = jnp.zeros((total_row_count, CH), jnp.float32)
    for kernel_tap_index in range(3):
        shifted_rows = padded_input_gradient[
            (2 - kernel_tap_index) * DILATION_STEP : (2 - kernel_tap_index) * DILATION_STEP
            + total_row_count
        ]
        dactivated = dactivated + lax.dot_general(
            shifted_rows,
            conv_weight[kernel_tap_index],
            contract_last,
            preferred_element_type=jnp.float32,
        )
    dnorm_path = jax.vjp(lambda values: activate(values, norm_gain), inputs)[1](dactivated)[0]
    input_grad = (dtower + dnorm_path).astype(jnp.bfloat16)
    channel_rows = CH // groups
    pieces = []
    for kernel_tap_index in range(3):
        tap_slice = kernel_tap_rows[kernel_tap_index]
        pieces.append(
            lax.dot_general(
                tap_slice, conv_output_gradient, contract_first, preferred_element_type=jnp.float32
            )
        )
    pieces.append(
        lax.dot_general(dtower_half, hidden, contract_first, preferred_element_type=jnp.float32)
    )
    local_sums = lax.psum_scatter(
        jnp.concatenate(pieces, axis=1).astype(jnp.bfloat16), "seq", scatter_dimension=0, tiled=True
    ).astype(jnp.float32)
    batch_part = lax.psum_scatter(
        local_sums.reshape(channel_rows, 4, INNER).astype(jnp.bfloat16),
        "batch",
        scatter_dimension=2,
        tiled=True,
    ).astype(jnp.float32) / lax.axis_size("batch")
    conv_grad = batch_part[:, :3, :].transpose(1, 0, 2)
    mix_grad = batch_part[:, 3, :].T
    return (predictions[None], input_grad[None], conv_grad, mix_grad)


def solution(mesh):
    in_specs = (
        P("batch", "seq", None),
        P(),
        P(None, "seq", "batch"),
        P("batch", "seq"),
        P(None, "seq"),
        P(),
        P("batch", "seq", None),
    )
    out_specs = (
        P("batch", "seq", None),
        P("batch", "seq", None),
        P(None, "seq", "batch"),
        P("batch", "seq"),
    )
    return jax.shard_map(body, mesh=mesh, in_specs=in_specs, out_specs=out_specs, check_vma=False)
```

profile of v0, /device:TPU:8, one launch (start us, length us, event | category | flops | bytes accessed | tf_op | source)
XLA Modules:
  0.0 487.8 jit_solution(11521430393118905117)
XLA Ops:
  7.2 0.0 copy-start
  7.2 0.0 all-gather.4.cloned.1.call-start
  7.2 52.3 %all_gather.15 = bf16[3,96,768]{1,2,0:T(8,128)(2,1)S(1)} all-gather(bf16[3,96,48]{1,2,0:T(8,128)(2,1)} %param.9), channel_id=1, replica_groups=mesh['batch'=16,'seq'=16] {'batch'}, dimensions={2}, use_global_device_ids=true | all-gather | bytes 470016 | tf_op jit(solution)/shard_map/all_gather | solution.py:41
  59.5 1.0 copy.17
  60.6 0.0 all-gather.4.cloned.1.call-update
  60.6 0.0 all-gather.6.cloned.1.call-start
  60.6 39.4 %all_gather.17 = bf16[768,96]{1,0:T(8,128)(2,1)S(1)} all-gather(bf16[48,96]{1,0:T(8,128)(2,1)} %param.10), channel_id=1, replica_groups=mesh['batch'=16,'seq'=16] {'batch'}, dimensions={0}, use_global_device_ids=true | all-gather | bytes 156672 | tf_op jit(solution)/shard_map/all_gather | solution.py:42
  100.0 0.8 copy.18
  100.8 0.0 all-gather.6.cloned.1.call-update
  100.9 0.0 all-gather.8.cloned.1.call-start
  100.9 0.2 fusion.15
  101.1 0.4 fusion.22
  101.5 1.9 collective-permute-start
  103.4 3.6 collective-permute-start.1
  107.1 0.0 all-gather.4.cloned.1.call-done
  107.1 2.4 fusion.6
  109.5 0.0 collective-permute-done.1
  109.5 2.1 fusion.8
  111.7 0.0 collective-permute-done
  111.7 2.1 fusion.10
  113.8 0.0 copy-start.4
  113.9 30.7 %all-gather.6.cloned.1.call-done = bf16[768,1536]{0,1:T(8,128)(2,1)} async-done(((bf16[768,96]{0,1:T(8,128)(2,1)}), bf16[768,1536]{0,1:T(8,128)(2,1)}) %all-gather.6.cloned.1.call-update) | async-done | bytes 2359312 | tf_op jit(solution)/shard_map/all_gather | solution.py:46
  144.5 3.3 fusion.1
  147.8 0.0 all-gather.8.cloned.1.call-update
  147.9 0.2 copy.23
  148.1 1.3 copy.20
  149.4 4.6 all-to-all-start.1
  154.1 0.0 reduce-scatter.6.cloned.1.call-start
  154.1 0.8 dynamic_slice.3
  154.9 14.0 %all-to-all-done.1 = bf16[128,16,256]{2,0,1:T(8,128)(2,1)S(1)} async-done(((bf16[128,16,256]{2,0,1:T(8,128)(2,1)}), bf16[128,16,256]{2,0,1:T(8,128)(2,1)S(1)}, u32[]{:S(2)}, u32[]{:S(2)}) %all-to-all-start.1) | async-done | bytes 1048608 | tf_op jit(solution)/shard_map/all_to_all | solution.py:82
  168.9 30.2 %all-gather.8.cloned.1.call-done = bf16[2048,1536]{1,0:T(8,128)(2,1)} async-done(((bf16[128,1536]{1,0:T(8,128)(2,1)}), bf16[2048,1536]{1,0:T(8,128)(2,1)}) %all-gather.8.cloned.1.call-update) | async-done | bytes 6291472 | tf_op jit(solution)/shard_map/all_gather | solution.py:74
  199.1 6.8 %fusion.3 = (bf16[2048,256]{1,0:T(8,128)(2,1)S(1)}, bf16[2048,256]{1,0:T(8,128)(2,1)}) fusion(bf16[128,16,256]{2,0,1:T(8,128)(2,1)S(1)} %all-to-all-done.1, f32[256]{0:T(256)S(1)} %dynamic_slice.3, bf16[2048,1536]{1,0:T(8,128)(2,1)} %all-gather.8.cloned.1.call-done, bf16[1536,256]{1,0:T(8,128)(2,1)S(1)} %copy-done), kind=kOutput, calls=%fused_computation.17 | convolution fusion | flops 1617952768 | bytes 10224640 | tf_op jit(solution)/shard_map/dot_general | solution.py:73
  205.9 4.5 convolution_convert_fusion
  210.4 0.0 reduce-scatter.6.cloned.1.call-update
  210.5 0.2 reduce-scatter.10.cloned.1.call-start
  210.7 69.3 %reduce-scatter.6.cloned.1.call-done = bf16[128,1536]{1,0:T(8,128)(2,1)} async-done(((bf16[2048,1536]{1,0:T(8,128)(2,1)}), bf16[128,1536]{1,0:T(8,128)(2,1)}) %reduce-scatter.6.cloned.1.call-update) | async-done | bytes 393232 | tf_op jit(solution)/shard_map/reduce_scatter | solution.py:84
  280.0 2.4 fusion.47
  282.5 0.8 convolution_convert_fusion.3
  283.3 0.2 copy-done.3
  283.5 0.8 convolution_convert_fusion.1
  284.3 0.8 convolution_convert_fusion.4
  285.2 0.8 convolution_convert_fusion.2
  286.0 4.5 pad_maximum_fusion
  290.4 12.7 %copy.21 = bf16[1536,3072]{1,0:T(8,128)(2,1)} copy(bf16[1536,3072]{0,1:T(8,128)(2,1)} %pad_maximum_fusion) | data formatting | bytes 18874368
  303.2 0.0 reduce-scatter.10.cloned.1.call-update
  303.2 0.0 reduce-scatter.8.cloned.1.call-start
  303.2 1.1 copy-done.5
  304.4 22.3 %all_to_all.29 = bf16[16,128,256]{2,1,0:T(8,128)(2,1)S(1)} all-to-all(bf16[16,128,256]{2,1,0:T(8,128)(2,1)S(1)} %bitcast.123), channel_id=1, replica_groups=mesh['batch'=16,'seq'=16] {'seq'}, dimensions={0} | all-to-all | bytes 2097152 | tf_op jit(solution)/shard_map/all_to_all | solution.py:81
  326.7 0.6 copy.19
  327.3 1.3 broadcast_in_dim.6
  328.6 6.0 %collective-permute-start.2 = (bf16[8,768]{1,0:T(8,128)(2,1)S(1)}, bf16[8,768]{1,0:T(8,128)(2,1)S(1)}, u32[]{:S(2)}, u32[]{:S(2)}) collective-permute-start(bf16[8,768]{1,0:T(8,128)(2,1)S(1)} %get-tuple-element.8), channel_id=1, source_target_pairs={{1,0},{2,1},{3,2},{4,3},{5,4},{6,5},{7,6},{8,7},{9,8},{10,9},{11,1... | collective-permute-start | bytes 36872 | tf_op jit(solution)/shard_map/ppermute | solution.py:21
  334.7 1.9 collective-permute-start.3
  336.6 3.5 fusion.5
  340.1 3.5 fusion.7
  343.5 42.8 %reduce-scatter.10.cloned.1.call-done = bf16[96,3072]{1,0:T(8,128)(2,1)} async-done(((bf16[1536,3072]{1,0:T(8,128)(2,1)}), bf16[96,3072]{1,0:T(8,128)(2,1)}) %reduce-scatter.10.cloned.1.call-update) | async-done | bytes 589840
  386.3 2.2 copy.22
  388.5 0.0 reduce-scatter.8.cloned.1.call-update
  388.6 0.0 copy-start.1
  388.6 3.5 fusion.25
  392.1 1.0 fusion.48
  393.1 85.8 %reduce-scatter.8.cloned.1.call-done = bf16[96,4,48]{0,2,1:T(8,128)(2,1)} async-done(((bf16[96,4,768]{0,2,1:T(8,128)(2,1)}), bf16[96,4,48]{0,2,1:T(8,128)(2,1)}) %reduce-scatter.8.cloned.1.call-update) | async-done | bytes 36880 | tf_op jit(solution)/shard_map/reduce_scatter | solution.py:127
  478.8 0.8 convert_multiply_fusion.1
  479.7 0.6 slice_bitcast_fusion.16
  480.3 0.6 slice_bitcast_fusion.15
  (15 shorter events, 0.1 us)
Async XLA Ops:
  7.2 191.9 %copy-start = (bf16[1536,256]{1,0:T(8,128)(2,1)S(1)}, bf16[1536,256]{1,0:T(8,128)(2,1)}, u32[]{:S(2)}) copy-start(bf16[1536,256]{1,0:T(8,128)(2,1)} %param.11) | copy-start | bytes 2359300
  7.2 93.7 %copy-start.2 = (bf16[1,128,1536]{2,1,0:T(8,128)(2,1)S(1)}, bf16[1,128,1536]{2,1,0:T(8,128)(2,1)}, u32[]{:S(2)}) copy-start(bf16[1,128,1536]{2,1,0:T(8,128)(2,1)} %param.7) | copy-start | bytes 1179652
  7.2 93.9 %copy-start.6 = (f32[1536]{0:T(1024)S(1)}, f32[1536]{0:T(1024)}, u32[]{:S(2)}) copy-start(f32[1536]{0:T(1024)} %param.8) | copy-start | bytes 18436
  7.2 99.9 %all-gather.4.cloned.1.call-start = ((), (), s32[]{:S(2)}) async-start(), calls=%async_computation.5 | async-start | bytes 7520256 | tf_op jit(solution)/shard_map/all_gather | solution.py:45
  60.6 84.0 %all-gather.6.cloned.1.call-start = ((), (), s32[]{:S(2)}) async-start(), calls=%async_computation.6 | async-start | bytes 2506752 | tf_op jit(solution)/shard_map/all_gather | solution.py:46
  100.9 98.2 %all-gather.8.cloned.1.call-start = ((), (), s32[]{:S(2)}) async-start(), calls=%async_computation.7 | async-start | bytes 6684672 | tf_op jit(solution)/shard_map/all_gather | solution.py:74
  101.5 10.2 %collective-permute-start = (bf16[8,1536]{1,0:T(8,128)(2,1)S(1)}, bf16[8,1536]{1,0:T(8,128)(2,1)S(1)}, u32[]{:S(2)}, u32[]{:S(2)}) collective-permute-start(bf16[8,1536]{1,0:T(8,128)(2,1)S(1)} %get-tuple-element.6), channel_id=1, source_target_pairs={{0,1},{1,2},{2,3},{3,4},{4,5},{5,6},{6,7},{7,8},{8,9},{9,10},{10,1... | collective-permute-start | bytes 73736 | tf_op jit(solution)/shard_map/ppermute | solution.py:19
  103.4 6.1 %collective-permute-start.1 = (bf16[8,1536]{1,0:T(8,128)(2,1)S(1)}, bf16[8,1536]{1,0:T(8,128)(2,1)S(1)}, u32[]{:S(2)}, u32[]{:S(2)}) collective-permute-start(bf16[8,1536]{1,0:T(8,128)(2,1)S(1)} %get-tuple-element.7), channel_id=1, source_target_pairs={{1,0},{2,1},{3,2},{4,3},{5,4},{6,5},{7,6},{8,7},{9,8},{10,9},{11,1... | collective-permute-start | bytes 73736 | tf_op jit(solution)/shard_map/ppermute | solution.py:21
  113.8 34.0 %copy-start.4 = (bf16[1,128,4096]{2,1,0:T(8,128)(2,1)S(1)}, bf16[1,128,4096]{2,1,0:T(8,128)(2,1)}, u32[]{:S(2)}) copy-start(bf16[1,128,4096]{2,1,0:T(8,128)(2,1)} %param.13) | copy-start | bytes 3145732
  149.4 19.4 %all-to-all-start.1 = ((bf16[128,16,256]{2,0,1:T(8,128)(2,1)}), bf16[128,16,256]{2,0,1:T(8,128)(2,1)S(1)}, u32[]{:S(2)}, u32[]{:S(2)}) async-start(bf16[128,16,256]{2,0,1:T(8,128)(2,1)} %copy.20), calls=%async_computation.1 | async-start | bytes 2097152 | tf_op jit(solution)/shard_map/all_to_all | solution.py:82
  154.1 126.0 %reduce-scatter.6.cloned.1.call-start = ((), (), s32[]{:S(2)}) async-start(), calls=%async_computation.8 | async-start | bytes 6684672 | tf_op jit(solution)/shard_map/reduce_scatter | solution.py:84
  210.5 175.8 %reduce-scatter.10.cloned.1.call-start = ((), (), s32[]{:S(2)}) async-start(), calls=%async_computation.10 | async-start | bytes 10027008
  282.5 1.0 copy-start.3
  303.2 1.2 copy-start.5
  303.2 175.7 %reduce-scatter.8.cloned.1.call-start = ((), (), s32[]{:S(2)}) async-start(), calls=%async_computation.9 | async-start | bytes 835584 | tf_op jit(solution)/shard_map/reduce_scatter | solution.py:127
  328.6 59.9 %collective-permute-start.2 = (bf16[8,768]{1,0:T(8,128)(2,1)S(1)}, bf16[8,768]{1,0:T(8,128)(2,1)S(1)}, u32[]{:S(2)}, u32[]{:S(2)}) collective-permute-start(bf16[8,768]{1,0:T(8,128)(2,1)S(1)} %get-tuple-element.8), channel_id=1, source_target_pairs={{1,0},{2,1},{3,2},{4,3},{5,4},{6,5},{7,6},{8,7},{9,8},{10,9},{11,1... | collective-permute-start | bytes 36872 | tf_op jit(solution)/shard_map/ppermute | solution.py:21
  334.7 5.4 %collective-permute-start.3 = (bf16[8,768]{1,0:T(8,128)(2,1)S(1)}, bf16[8,768]{1,0:T(8,128)(2,1)S(1)}, u32[]{:S(2)}, u32[]{:S(2)}) collective-permute-start(bf16[8,768]{1,0:T(8,128)(2,1)S(1)} %get-tuple-element.9), channel_id=1, source_target_pairs={{0,1},{1,2},{2,3},{3,4},{4,5},{5,6},{6,7},{7,8},{8,9},{9,10},{10,1... | collective-permute-start | bytes 36872 | tf_op jit(solution)/shard_map/ppermute | solution.py:19
  388.6 92.4 %copy-start.1 = (bf16[1536,256]{1,0:T(8,128)(2,1)S(1)}, bf16[1536,256]{1,0:T(8,128)(2,1)}, u32[]{:S(2)}) copy-start(bf16[1536,256]{1,0:T(8,128)(2,1)} %param.11) | copy-start | bytes 2359300
Sparse Core Ops, SparseCore 0:
  60.7 43.3 all-gather.3
  106.5 38.0 all-gather.5
  148.0 51.0 all-gather.7
  210.6 69.4 reduce-scatter.5
  303.3 82.9 reduce-scatter.9
  389.6 89.1 reduce-scatter.7
where the time goes:
time: 489 us; the launch traced here: 488 us
  waiting for transfers between devices  273 us (56%)
  blocking collectives  114 us (23%)
  matrix products  37.5 us (8%)
  local copies, waits for them, and re-layouts  23.5 us (5%)
  starting transfers between devices  18.6 us (4%)
  between operations  14.3 us (3%)
  other arithmetic  6.87 us (1%)
    reduce_scatter x1, waiting for transfers between devices, body(): lax.psum_scatter(local_sums.reshape(channel_rows, 4, INNER).astype(jnp.bf...  85.8 us
    reduce_scatter x1, waiting for transfers between devices, body(): lax.psum_scatter(lax.dot_general(dlogits, head_weight, contract_last, pre...  69.3 us
    all_gather x1, blocking collectives, body(): lax.all_gather(conv_weight, 'batch', axis=2, tiled=True)  52.3 us
    unnamed x7, waiting for transfers between devices  42.9 us
    all_gather x1, blocking collectives, body(): lax.all_gather(mix_weight, 'batch', axis=0, tiled=True)  39.4 us
    all_gather x1, waiting for transfers between devices, body(): lax.all_gather(mix_part_w, 'seq', axis=1, tiled=True)  30.7 us
    all_gather x1, waiting for transfers between devices, body(): lax.all_gather(tower_out, 'seq', axis=0, tiled=True)  30.2 us
    all_to_all x1, blocking collectives, body(): lax.all_to_all(pred_local, 'seq', split_axis=0, concat_axis=1, tiled=True)  22.3 us
  transfers between devices with their start and end apart: 11, of which 6 were waited for; matrix products, arithmetic and copies ran while one was open for 5% of the time, Pallas kernels for 0%

commit v1 on v0

v1 whole, which is shorter than its diff:
```python
import functools

import jax
import jax.numpy as jnp
from jax import lax
from jax.experimental import pallas as pl
from jax.experimental.pallas import tpu as pltpu
from jax.sharding import PartitionSpec as P

CH = 1536
INNER = 768
TRACKS = 4096
STEP = 8
BINS = 128
BF16 = jnp.bfloat16
F32 = jnp.float32
ROOT = 0.7978845608028654
CUBE = 0.044715
LAST = (((1,), (1,)), ((), ()))
N_COPIES = 260


def place():
    b, s = lax.axis_index("batch"), lax.axis_index("seq")
    return b % 4, (s // 2) % 4, (b // 4) * 2 + s // 8, s % 2


def device(x, y, z, c):
    return ((z // 2) * 4 + x, (z % 2) * 8 + y * 2 + c)


class Copies:
    def __init__(self, send, recv):
        self.send, self.recv, self.sent, self.ids = send, recv, [], {}

    def of(self, src, dst, to, key):
        i = self.ids.setdefault(key, len(self.ids))
        return pltpu.make_async_remote_copy(
            src_ref=src,
            dst_ref=dst,
            send_sem=self.send.at[i],
            recv_sem=self.recv.at[i],
            device_id=to,
            device_id_type=pl.DeviceIdType.MESH,
        )

    def start(self, block, to, key, dst=None):
        copy = self.of(block, block if dst is None else dst, to, key)
        copy.start()
        self.sent.append(copy)

    def arrive(self, block, to, key):
        self.of(block, block, to, key).wait_recv()

    def finish(self):
        for copy in self.sent:
            copy.wait_send()


def meet(x, y, z, c):
    b, s = lax.axis_index("batch"), lax.axis_index("seq")
    others = [device(x, y, z, 1 - c), (b, (s + 1) % 16), (b, (s + 15) % 16)]
    others += [device((x + d) % 4, y, z, c) for d in (1, 2, 3)]
    others += [device(x, (y + d) % 4, z, c) for d in (1, 2, 3)]
    others += [device(x, y, (z + d) % 8, c) for d in range(1, 8)]
    barrier = pltpu.get_barrier_semaphore()
    for other in others:
        pl.semaphore_signal(barrier, inc=1, device_id=other, device_id_type=pl.DeviceIdType.MESH)
    pl.semaphore_wait(barrier, len(others))


def gelu(v):
    return 0.5 * v * (1.0 + jnp.tanh(ROOT * (v + CUBE * v * v * v)))


def gelu_slope(v):
    t = jnp.tanh(ROOT * (v + CUBE * v * v * v))
    return 0.5 * (1.0 + t) + 0.5 * v * (1.0 - t * t) * (ROOT * (1.0 + 3.0 * CUBE * v * v))


def rows_loop(total, step):
    def run(body):
        def one(i, carry):
            body(pl.multiple_of(i * step, step))
            return carry

        lax.fori_loop(0, total // step, one, 0)

    return run


def kernel(
    shard_ref, h_ref, in_ref, gain_ref, bias_ref, cot_ref,
    pred_ref, ig_ref, grad_ref,
    W, H, act, AP, AX, conv, hidden, tower, dtower, DT, DX, dext, dext16, hT, dT, dh2, dact,
    G, RX, RY, RZ, M0, M1, M2, L0, L1, L2, sum0,
    send, recv, local,
):
    x, y, z, c = place()
    b, s = lax.axis_index("batch"), lax.axis_index("seq")
    zl, zh = z % 2, z // 2
    sib = device(x, y, z, 1 - c)
    before, after = (b, (s + 15) % 16), (b, (s + 1) % 16)
    own = [
        pltpu.make_async_copy(shard_ref, W.at[:, zl, y, c, zh, x], local.at[0]),
        pltpu.make_async_copy(h_ref, H.at[zl, y, c], local.at[1]),
    ]
    for copy in own:
        copy.start()
    meet(x, y, z, c)
    copies = Copies(send, recv)
    start, arrive = copies.start, copies.arrive

    def at(dx=0, dy=0, dz=0):
        return device((x + dx) % 4, (y + dy) % 4, (z + dz) % 8, c)

    def shard(dz):
        zz = (z + dz) % 8
        return W.at[:, zz % 2, y, c, zz // 2, x]

    def col(part, dx, dy):
        parts = pl.ds(0, 2) if part == 0 else pl.ds(2, 1)
        return W.at[parts, :, (y + dy) % 4, c, :, (x + dx) % 4]

    def half_col(part, dx, dy, half):
        if part == 0:
            return W.at[half, :, (y + dy) % 4, c, :, (x + dx) % 4]
        return W.at[2, half, (y + dy) % 4, c, :, (x + dx) % 4]

    def head(dzl, dy, half):
        rows = slice(None) if half is None else pl.ds(half * 768, 768)
        return H.at[(zl + dzl) % 2, (y + dy) % 4, c, rows]

    def spread(d):
        start(col(0, 0, d), at(dx=1), ("p3", 0, 1, d % 4))
        start(col(0, 0, d), at(dx=-1), ("p3", 0, 3, d % 4))
        start(col(1, d, 0), at(dy=1), ("p3", 1, 1, d % 4))
        start(col(1, d, 0), at(dy=-1), ("p3", 1, 3, d % 4))
        start(col(0, 0, d), sib, ("s", 0, 0, d % 4))
        start(col(1, d, 0), sib, ("s", 1, 0, d % 4))

    def second_hop(q):
        for d in (1, -1):
            half = 0 if d == 1 else 1
            arrive(col(0, -d, q), sib, ("p3", 0, d % 4, q % 4))
            start(half_col(0, -d, q, half), at(dx=d), ("p4", 0, d % 4, q % 4))
            start(col(0, -d, q), sib, ("s", 0, d % 4, q % 4))
            arrive(col(1, q, -d), sib, ("p3", 1, d % 4, q % 4))
            start(half_col(1, q, -d, half), at(dy=d), ("p4", 1, d % 4, q % 4))
            start(col(1, q, -d), sib, ("s", 1, d % 4, q % 4))

    def last_hop(q):
        for half, d in ((0, 1), (1, -1)):
            arrive(half_col(0, 2, q, half), sib, ("p4", 0, d % 4, q % 4))
            arrive(half_col(1, q, 2, half), sib, ("p4", 1, d % 4, q % 4))
        start(col(0, 2, q), sib, ("s", 0, 2, q % 4))
        start(col(1, q, 2), sib, ("s", 1, 2, q % 4))

    def head_first():
        for d, half in ((1, 0), (-1, 1)):
            arrive(head(0, -d, half), sib, ("hy", d % 4, half))
            start(head(0, -d, half), at(dy=d), ("hy2", d % 4))
            start(head(0, -d, half), at(dz=d), ("hz", d % 8, -d % 4))

    def head_second():
        for d, half in ((1, 0), (-1, 1)):
            arrive(head(0, -d, 1 - half), sib, ("hy", d % 4, 1 - half))
            start(head(0, -d, 1 - half), at(dz=-d), ("hz", -d % 8, -d % 4))
            start(head(0, -d, None), sib, ("hs", 0, -d % 4))

    def head_third():
        arrive(head(0, 2, 0), sib, ("hy2", 1))
        arrive(head(0, 2, 1), sib, ("hy2", 3))
        start(head(0, 2, 0), at(dz=1), ("hz", 1, 2))
        start(head(0, 2, 1), at(dz=-1), ("hz", 7, 2))
        start(head(0, 2, None), sib, ("hs", 0, 2))

    def head_other(dy):
        arrive(head(1, dy, 0), sib, ("hz", 1, dy % 4))
        arrive(head(1, dy, 1), sib, ("hz", 7, dy % 4))
        start(head(1, dy, None), sib, ("hs", 1, dy % 4))

    def from_sib():
        for q in (0, -1, 1, 2):
            for d in (0, 1, -1, 2):
                arrive(W.at[pl.ds(0, 2), :, (y + q) % 4, 1 - c, :, (x - d) % 4], sib, ("s", 0, d % 4, q % 4))
                arrive(W.at[pl.ds(2, 1), :, (y - d) % 4, 1 - c, :, (x + q) % 4], sib, ("s", 1, d % 4, q % 4))

    own[0].wait()
    for dz in (1, -1, 2, -2, 3, -3, 4):
        start(shard(0), at(dz=dz), ("z", dz % 8))
    own[1].wait()
    for half in (0, 1):
        start(head(0, 0, half), at(dy=1), ("hy", 1, half))
        start(head(0, 0, 1 - half), at(dy=-1), ("hy", 3, 1 - half))
    start(head(0, 0, None), sib, ("hs", 0, 0))

    @rows_loop(BINS, 16)
    def _(r):
        v = in_ref[pl.ds(r, 16), :].astype(F32)
        mean_sq = jnp.mean(v * v, axis=-1, keepdims=True)
        a = gelu(v * lax.rsqrt(mean_sq + 1e-06) * gain_ref[...])
        act[pl.ds(r + 8, 16), :] = a.astype(BF16).astype(F32)

    start(act.at[pl.ds(8, 8)], before, ("halo", 0), dst=act.at[pl.ds(136, 8)])
    start(act.at[pl.ds(128, 8)], after, ("halo", 1), dst=act.at[pl.ds(0, 8)])

    for dz in (1, -1, 2, -2, 3, -3, 4):
        arrive(shard(-dz), sib, ("z", dz % 8))
    for d in (1, -1, 2):
        start(col(0, 0, 0), at(dy=d), ("p2", 0, d % 4))
        start(col(1, 0, 0), at(dx=d), ("p2", 1, d % 4))
    spread(0)
    start(head(0, 0, 0), at(dz=1), ("hz", 1, 0))
    start(head(0, 0, 1), at(dz=-1), ("hz", 7, 0))
    for d in (1, -1):
        arrive(col(0, 0, -d), sib, ("p2", 0, d % 4))
        arrive(col(1, -d, 0), sib, ("p2", 1, d % 4))
        spread(-d)
    arrive(act.at[pl.ds(136, 8)], sib, ("halo", 0))
    arrive(act.at[pl.ds(0, 8)], sib, ("halo", 1))

    @pl.when(s == 0)
    def _():
        act[0:8, :] = jnp.zeros((8, CH), F32)

    @pl.when(s == 15)
    def _():
        act[136:144, :] = jnp.zeros((8, CH), F32)

    arrive(col(0, 0, 2), sib, ("p2", 0, 2))
    arrive(col(1, 2, 0), sib, ("p2", 1, 2))
    spread(2)
    head_first()

    @rows_loop(BINS, 16)
    def _(r):
        for q in range(4):
            taps = [act[pl.ds(r + 8 * k, 16), pl.ds(q * 384, 384)] for k in range(3)]
            for i in range(4):
                g = 4 * q + i
                pieces = [t[:, 96 * i : 96 * i + 96] for t in taps] + [jnp.zeros((16, 96), F32)]
                AP[g % 2, g // 2, pl.ds(r, 16), :] = jnp.concatenate(pieces, axis=1).astype(BF16)

    start(AP.at[1 - c], sib, ("ax",), dst=AX)
    second_hop(0)
    second_hop(-1)
    head_second()
    second_hop(1)
    second_hop(2)
    for q in (0, -1, 1, 2):
        last_hop(q)
    head_third()
    from_sib()

    def w(p, j, cc):
        return W[p, j // 4, j % 4, cc].reshape(INNER, 128)

    conv[...] = jnp.zeros_like(conv)

    def conv_step(j, carry):
        lhs = jnp.concatenate([AP[0, j], AP[1, j]], axis=1)
        rhs = jnp.concatenate([w(p, j, cc) for cc in range(2) for p in range(3)], axis=1)
        conv[...] += lax.dot_general(lhs, rhs, LAST, preferred_element_type=F32)
        return carry

    lax.fori_loop(0, 8, conv_step, 0)
    for dy in (0, -1, 1, 2):
        head_other(dy)

    @rows_loop(BINS, 16)
    def _(r):
        hidden[pl.ds(r, 16), :] = gelu(conv[pl.ds(r, 16), :]).astype(BF16)

    start(hidden, sib, ("hidden",), dst=dh2.at[0])

    for q in range(4):
        mixed = []
        for i in range(2):
            j = 2 * q + i
            rhs = jnp.concatenate([w(2, j, 0), w(2, j, 1)], axis=1)
            m = jnp.dot(hidden[...], rhs, preferred_element_type=F32)
            mixed += [m[:, 32:128], m[:, 160:256]]
        lanes = slice(384 * q, 384 * q + 384)
        tower[:, lanes] = (in_ref[:, lanes].astype(F32) + jnp.concatenate(mixed, axis=1)).astype(BF16)

    dtower[...] = jnp.zeros_like(dtower)

    def head_step(zz, yy, cc):
        lanes = pl.ds(pl.multiple_of((zz * 8 + yy * 2 + cc) * 256, 256), 256)
        weight = H[zz, yy, cc]
        logits = jnp.dot(tower[...], weight, preferred_element_type=F32) + bias_ref[:, lanes]
        e = jnp.exp(-jnp.abs(logits))
        pred_ref[:, lanes] = (jnp.maximum(logits, 0.0) + jnp.log1p(e)).astype(BF16)
        sigmoid = jnp.where(logits >= 0.0, 1.0, e) / (1.0 + e)
        dlogits = (cot_ref[:, lanes].astype(F32) * sigmoid).astype(BF16)
        dtower[...] += lax.dot_general(dlogits, weight, LAST, preferred_element_type=F32)

    for cc in (0, 1):
        for dzl in (0, 1):
            for dy in (0, -1, 1, 2):
                piece = H.at[(zl + dzl) % 2, (y + dy) % 4, (c + cc) % 2]
                if cc == 1:
                    arrive(piece, sib, ("hs", dzl, dy % 4))

    def head_loop(g, carry):
        head_step(g // 8, (g // 2) % 4, g % 2)
        return carry

    lax.fori_loop(0, 16, head_loop, 0)

    @rows_loop(BINS, 16)
    def _(r):
        for q in range(4):
            v = dtower[pl.ds(r, 16), pl.ds(q * 384, 384)]
            for i in range(4):
                g = 4 * q + i
                pieces = [jnp.zeros((16, 32), F32), v[:, 96 * i : 96 * i + 96]]
                DT[g % 2, g // 2, pl.ds(r, 16), :] = jnp.concatenate(pieces, axis=1).astype(BF16)

    start(DT.at[1 - c], sib, ("dt",), dst=DX)
    sum0[...] = jnp.zeros_like(sum0)

    def dhidden_step(j, carry):
        lhs = jnp.concatenate([DT[0, j], DT[1, j]], axis=1)
        rhs = jnp.concatenate([w(2, j, 0), w(2, j, 1)], axis=1)
        sum0[...] += lax.dot_general(lhs, rhs, LAST, preferred_element_type=F32)
        return carry

    lax.fori_loop(0, 8, dhidden_step, 0)

    @rows_loop(BINS, 16)
    def _(r):
        d = sum0[pl.ds(r, 16), :] * gelu_slope(conv[pl.ds(r, 16), :])
        half = d.astype(BF16)
        dh2[2, pl.ds(r, 16), :] = half
        dext[pl.ds(r + 8, 16), :] = half.astype(F32)

    start(dh2.at[2], sib, ("dconv",), dst=dh2.at[1])
    start(dext.at[pl.ds(8, 8)], before, ("dhalo", 0), dst=dext.at[pl.ds(136, 8)])
    start(dext.at[pl.ds(128, 8)], after, ("dhalo", 1), dst=dext.at[pl.ds(0, 8)])

    arrive(dh2.at[0], sib, ("hidden",))
    arrive(dh2.at[1], sib, ("dconv",))
    arrive(AX, sib, ("ax",))
    arrive(DX, sib, ("dt",))
    hT[:, 0:128] = hidden[...].T
    hT[:, 128:256] = dh2[0].T
    dT[:, 0:128] = dh2[2].T
    dT[:, 128:256] = dh2[1].T

    def grad_step(j, carry):
        rhs = jnp.concatenate([AP[c, j], AX[j]], axis=0)
        g = jnp.dot(dT[...], rhs, preferred_element_type=F32)
        more = jnp.dot(hT[...], jnp.concatenate([DT[c, j], DX[j]], axis=0), preferred_element_type=F32)
        for p in range(3):
            part = g[:, 128 * p : 128 * p + 128]
            if p == 2:
                part = part + more
            G[p, j // 4, j % 4] = part.astype(BF16).reshape(4, 4, 48, 128)
        return carry

    lax.fori_loop(0, 8, grad_step, 0)

    def dact_prepare():
        arrive(dext.at[pl.ds(136, 8)], sib, ("dhalo", 0))
        arrive(dext.at[pl.ds(0, 8)], sib, ("dhalo", 1))

        @pl.when(s == 0)
        def _():
            dext[0:8, :] = jnp.zeros((8, INNER), F32)

        @pl.when(s == 15)
        def _():
            dext[136:144, :] = jnp.zeros((8, INNER), F32)

        dext16[...] = dext[...].astype(BF16)

    def dact_part(q):
        pieces = []
        for i in range(2):
            j = 2 * q + i
            for cc in range(2):
                rhs = jnp.concatenate([w(p, j, cc) for p in range(3)], axis=1)
                d = jnp.dot(dext16[...], rhs, preferred_element_type=F32)
                pieces.append(d[16:144, 0:96] + d[8:136, 96:192] + d[0:128, 192:288])
        dact[:, 384 * q : 384 * q + 384] = jnp.concatenate(pieces, axis=1)

    def dact_finish():
        @rows_loop(BINS, 16)
        def _(r):
            v = in_ref[pl.ds(r, 16), :].astype(F32)
            rs = lax.rsqrt(jnp.mean(v * v, axis=-1, keepdims=True) + 1e-06)
            gain = gain_ref[...]
            dz = dact[pl.ds(r, 16), :] * gelu_slope(v * rs * gain) * gain
            dot = jnp.mean(dz * v, axis=-1, keepdims=True)
            ig = dtower[pl.ds(r, 16), :] + dz * rs - v * (rs * rs * rs * dot)
            ig_ref[pl.ds(r, 16), :] = ig.astype(BF16)

    jobs = [dact_prepare] + [functools.partial(dact_part, q) for q in range(4)] + [dact_finish]

    def half_x(m, h):
        return G.at[0, h, :, :, (x + m) % 4]

    def half_y(m, h):
        return G.at[1, h, (y + m) % 4]

    def half_z(m, h):
        zz = (z + m) % 8
        return G.at[2, zz % 2, pl.ds(2 * h, 2), zz // 2]

    def slots(ring):
        return [(0, m) for m in range(ring, 0, -1)], [(1, m) for m in range(ring - 1, 0, -1)]

    def order(n):
        seq = []
        for m in range(n // 2, 0, -1):
            seq.append((0, m))
            if m > 1:
                seq.append((1, m - 1))
        return seq

    rings = {"x": (4, half_x, RX, "dx"), "y": (4, half_y, RY, "dy"), "z": (8, half_z, RZ, "dz")}

    def ring_send(ax, d, k):
        n, block, buf, name = rings[ax]
        h, m = order(n)[k]
        h = h if d < 0 else 1 - h
        start(block(d * m, h), at(**{name: d}), ("r" + ax, d, k), dst=buf.at[(d + 1) // 2, k])

    def add(dst, srcs):
        total = dst[...].astype(F32)
        for src in srcs:
            total = total + src[...].astype(F32)
        dst[...] = total.astype(BF16)

    def ring_receive(ax, d, k):
        n, block, buf, name = rings[ax]
        seq = order(n)
        h, m = seq[k]
        slot = buf.at[(d + 1) // 2, k]
        arrive(slot, sib, ("r" + ax, d, k))
        mine = h if d < 0 else 1 - h
        add(block(d * (m - 1), mine), [slot])
        if m > 1:
            ring_send(ax, d, seq.index((h, m - 1)))

    for ax in "xyz":
        for d in (-1, 1):
            ring_send(ax, d, 0)
            ring_send(ax, d, 1)
    jobs.pop(0)()
    jobs.pop(0)()

    def both(ax, k):
        for d in (-1, 1):
            ring_receive(ax, d, k)

    both("z", 0)
    both("x", 0)
    both("y", 0)
    both("z", 1)
    jobs.pop(0)()
    both("z", 2)
    both("x", 1)
    both("y", 1)
    both("z", 3)
    jobs.pop(0)()
    both("z", 4)
    both("x", 2)
    both("y", 2)

    def mid_send(p, d):
        if p == 0:
            start(G.at[0, :, (y + d) % 4, :, x], at(dy=d), ("m", 0, d), dst=M0.at[d - 1])
        elif p == 1:
            start(G.at[1, :, y, :, (x + d) % 4], at(dx=d), ("m", 1, d), dst=M1.at[d - 1])
        else:
            start(G.at[2, zl, :, zh, (x + d) % 4], at(dx=d), ("m", 2, d), dst=M2.at[d - 1])

    def mid_receive(p):
        buf = (M0, M1, M2)[p]
        for d in (1, 2, 3):
            arrive(buf.at[d - 1], sib, ("m", p, d))
        home = (G.at[0, :, y, :, x], G.at[1, :, y, :, x], G.at[2, zl, :, zh, x])[p]
        add(home, [buf.at[d] for d in range(3)])

    for p in (0, 1):
        for d in (1, 2, 3):
            mid_send(p, d)
    both("z", 5)
    both("z", 6)
    for d in (1, 2, 3):
        mid_send(2, d)
    jobs.pop(0)()

    def last_send(p, d):
        if p < 2:
            zz = (z + d) % 8
            start(G.at[p, zz % 2, y, zz // 2, x], at(dz=d), ("l", p, d), dst=(L0, L1)[p].at[d - 1])
        else:
            start(G.at[2, zl, (y + d) % 4, zh, x], at(dy=d), ("l", 2, d), dst=L2.at[d - 1])

    def last_receive(p):
        buf, n = ((L0, 7), (L1, 7), (L2, 3))[p]
        for d in range(n):
            arrive(buf.at[d], sib, ("l", p, d + 1))
        total = G[p, zl, y, zh, x].astype(F32)
        for d in range(n):
            total = total + buf[d].astype(F32)
        grad_ref[p] = total * (1.0 / 16.0)

    for p in (0, 1):
        mid_receive(p)
        for d in range(1, 8):
            last_send(p, d)
    mid_receive(2)
    for d in (1, 2, 3):
        last_send(2, d)
    while jobs:
        jobs.pop(0)()
    for p in range(3):
        last_receive(p)
    copies.finish()
    assert len(copies.ids) <= N_COPIES, len(copies.ids)


def body(tower_input, norm_gain, conv_weight, mix_weight, head_weight, head_bias, pred_cotangent):
    shard = jnp.concatenate([conv_weight.transpose(2, 0, 1), mix_weight[:, None, :]], axis=1)
    shard = shard.reshape(48, 3, 128).transpose(1, 0, 2)
    vmem = pl.BlockSpec(memory_space=pltpu.VMEM)
    hbm = pl.BlockSpec(memory_space=pl.ANY)
    scratch = [
        ((3, 2, 4, 2, 4, 4, 48, 128), BF16),
        ((2, 4, 2, CH, 256), BF16),
        ((BINS + 16, CH), F32),
        ((2, 8, BINS, 384), BF16),
        ((8, BINS, 384), BF16),
        ((BINS, INNER), F32),
        ((BINS, INNER), BF16),
        ((BINS, CH), BF16),
        ((BINS, CH), F32),
        ((2, 8, BINS, 128), BF16),
        ((8, BINS, 128), BF16),
        ((BINS + 16, INNER), F32),
        ((BINS + 16, INNER), BF16),
        ((INNER, 256), BF16),
        ((INNER, 256), BF16),
        ((3, BINS, INNER), BF16),
        ((BINS, CH), F32),
        ((3, 2, 4, 4, 4, 48, 128), BF16),
        ((2, 3, 4, 4, 48, 128), BF16),
        ((2, 3, 4, 4, 48, 128), BF16),
        ((2, 7, 2, 4, 48, 128), BF16),
        ((3, 2, 4, 48, 128), BF16),
        ((3, 2, 4, 48, 128), BF16),
        ((3, 4, 48, 128), BF16),
        ((7, 48, 128), BF16),
        ((7, 48, 128), BF16),
        ((3, 48, 128), BF16),
        ((BINS, INNER), F32),
    ]
    predictions, input_grad, grads = pl.pallas_call(
        kernel,
        out_shape=[
            jax.ShapeDtypeStruct((BINS, TRACKS), BF16),
            jax.ShapeDtypeStruct((BINS, CH), BF16),
            jax.ShapeDtypeStruct((3, 48, 128), F32),
        ],
        in_specs=[hbm, hbm, vmem, vmem, vmem, vmem],
        out_specs=[vmem, vmem, vmem],
        scratch_shapes=[pltpu.VMEM(*spec) for spec in scratch]
        + [
            pltpu.SemaphoreType.DMA((N_COPIES,)),
            pltpu.SemaphoreType.DMA((N_COPIES,)),
            pltpu.SemaphoreType.DMA((2,)),
        ],
        compiler_params=pltpu.CompilerParams(
            collective_id=0, has_side_effects=True, vmem_limit_bytes=60 * 2**20
        ),
        name="block",
    )(
        shard,
        head_weight,
        tower_input[0],
        norm_gain.reshape(1, CH),
        head_bias.reshape(1, TRACKS),
        pred_cotangent[0],
    )
    grads = grads.transpose(1, 0, 2).reshape(48, 4, 96)
    conv_grad = grads[:, :3].transpose(1, 2, 0)
    mix_grad = grads[:, 3]
    return (predictions[None], input_grad[None], conv_grad, mix_grad)


def solution(mesh):
    in_specs = (
        P("batch", "seq", None),
        P(),
        P(None, "seq", "batch"),
        P("batch", "seq"),
        P(None, "seq"),
        P(),
        P("batch", "seq", None),
    )
    out_specs = (
        P("batch", "seq", None),
        P("batch", "seq", None),
        P(None, "seq", "batch"),
        P("batch", "seq"),
    )
    return jax.shard_map(body, mesh=mesh, in_specs=in_specs, out_specs=out_specs, check_vma=False)
```

time: 489 us -> 133 us (0.27)
  waiting for transfers between devices: 273 us -> 0 us
  Pallas kernels: 0 us -> 124 us
  blocking collectives: 114 us -> 0 us
  matrix products: 37.5 us -> 0 us
  starting transfers between devices: 18.6 us -> 0 us
  local copies, waits for them, and re-layouts: 23.5 us -> 7.47 us
  between operations: 14.3 us -> 0.68 us
  other arithmetic: 6.87 us -> 0.78 us
    reduce_scatter x2 -> x0, waiting for transfers between devices: 155 us -> none  [the longest x1 85.8 us: body(): lax.psum_scatter(local_sums.reshape(channel_rows, 4, INNER).astype(jnp.bf...]
    pallas_call x0 -> x1, Pallas kernels: none -> 124 us  [body(): pl.pallas_call(kernel, out_shape=[jax.ShapeDtypeStruct((BINS, TRACKS), BF...]
    all_gather x2 -> x0, blocking collectives: 91.7 us -> none  [the longest x1 52.3 us: body(): lax.all_gather(conv_weight, 'batch', axis=2, tiled=True)]
    all_gather x3 -> x0, waiting for transfers between devices: 60.9 us -> none  [the longest x1 30.7 us: body(): lax.all_gather(mix_part_w, 'seq', axis=1, tiled=True)]
    unnamed x7 -> x0, waiting for transfers between devices: 42.9 us -> none
    dot_general x14 -> x0, matrix products: 37.5 us -> none  [the longest x3 10.4 us: body(): lax.dot_general(shifted_rows, conv_weight[kernel_tap_index], contract_las...]
    all_to_all x1 -> x0, blocking collectives: 22.3 us -> none  [body(): lax.all_to_all(pred_local, 'seq', split_axis=0, concat_axis=1, tiled=True)]
    all_to_all x1 -> x0, waiting for transfers between devices: 14 us -> none  [body(): lax.all_to_all(pred_cotangent[0], 'seq', split_axis=1, concat_axis=0, til...]
  transfers between devices with their start and end apart: 11 -> 0, of which waited for: 6 -> 0; matrix products, arithmetic and copies ran while one was open for 5% -> 0% of each run, Pallas kernels for 0% -> 0%
where the time goes in v1:
time: 133 us
  Pallas kernels  124 us (93%)
  local copies, waits for them, and re-layouts  7.47 us (6%)
    pallas_call x1, Pallas kernels, body(): pl.pallas_call(kernel, out_shape=[jax.ShapeDtypeStruct((BINS, TRACKS), BF...  124 us
    unnamed x7, local copies, waits for them, and re-layouts  3.73 us

profile of v1, /device:TPU:8, one launch (start us, length us, event | category | flops | bytes accessed | tf_op | source)
XLA Modules:
  0.0 133.0 jit_solution(349707673082657542)
XLA Ops:
  0.6 0.0 copy-start.1
  0.6 1.3 reshape.21.gain_ref
  1.9 0.0 copy-done.1
  1.9 0.8 pad_maximum_fusion
  2.8 0.1 reshape.20
  2.9 0.6 copy.16
  3.5 124.1 %block.1 = (bf16[128,4096]{1,0:T(8,128)(2,1)}, bf16[128,1536]{1,0:T(8,128)(2,1)}, f32[3,48,128]{2,1,0:T(8,128)}) custom-call(bf16[3,48,128]{2,1,0:T(8,128)(2,1)} %bitcast.18, bf16[1536,256]{1,0:T(8,128)(2,1)} %h_ref.1, bf16[128,1536]{1,0:T(8,128)(2,1)} %bitcast.17, f32[1,1536]{1,0:T(1,128)} %reshape.21.gain_ref, f32[1,4096]{1,0:T(1,128)} %bitcast.22, ...), custom_call_target="tpu_custom_call" | custom-call | tf_op jit(solution)/shard_map/block/pallas_call | solution.py:563
  127.6 0.9 copy.13
  128.5 0.1 reshape.23
  128.7 0.6 slice.9
  129.3 0.6 copy.14
  129.9 0.0 copy-start
  129.9 2.3 %copy.19 = bf16[1,128,4096]{2,1,0:T(8,128)(2,1)} copy(bf16[1,128,4096]{2,1,0:T(8,128)(2,1)} %bitcast.14) | data formatting | bytes 2097152
  132.3 0.0 copy-done
  132.3 0.7 copy.20
  (2 shorter events, 0.0 us)
Async XLA Ops:
  0.6 1.3 copy-start.1
  129.9 2.3 %copy-start = (bf16[128,1536]{1,0:T(8,128)(2,1)S(1)}, bf16[128,1536]{1,0:T(8,128)(2,1)}, u32[]{:S(2)}) copy-start(bf16[128,1536]{1,0:T(8,128)(2,1)} %get-tuple-element.8) | copy-start | bytes 1179652

commit v2 on v1

--- a/solution.py
+++ b/solution.py
@@ -17,7 +17,7 @@
 ROOT = 0.7978845608028654
 CUBE = 0.044715
 LAST = (((1,), (1,)), ((), ()))
-N_COPIES = 260
+N_COPIES = 137
 
 
 def place():
@@ -52,6 +52,9 @@
     def arrive(self, block, to, key):
         self.of(block, block, to, key).wait_recv()
 
+    def group(self, block, to, key):
+        self.of(block, block, to, key).start()
+
     def finish(self):
         for copy in self.sent:
             copy.wait_send()
@@ -90,10 +93,10 @@
 
 
 def kernel(
-    shard_ref, h_ref, in_ref, gain_ref, bias_ref, cot_ref,
-    pred_ref, ig_ref, grad_ref,
+    taps_ref, mix_ref, h_ref, in_ref, gain_ref, bias_ref, cot_ref,
+    pred_out, ig_ref, grad_ref,
     W, H, act, AP, AX, conv, hidden, tower, dtower, DT, DX, dext, dext16, hT, dT, dh2, dact,
-    G, RX, RY, RZ, M0, M1, M2, L0, L1, L2, sum0,
+    pred_ref, G, RX, RY, RZ, M0, M1, M2, L0, L1, L2, sum0,
     send, recv, local,
 ):
     x, y, z, c = place()
@@ -101,12 +104,13 @@
     zl, zh = z % 2, z // 2
     sib = device(x, y, z, 1 - c)
     before, after = (b, (s + 15) % 16), (b, (s + 1) % 16)
-    own = [
-        pltpu.make_async_copy(shard_ref, W.at[:, zl, y, c, zh, x], local.at[0]),
-        pltpu.make_async_copy(h_ref, H.at[zl, y, c], local.at[1]),
-    ]
-    for copy in own:
-        copy.start()
+    own = pltpu.make_async_copy(h_ref, H.at[zl, y, c], local.at[0])
+    own.start()
+    packed = [taps_ref[k].astype(F32) for k in range(3)] + [mix_ref[...].astype(F32)]
+    packed = jnp.concatenate(packed, axis=1).astype(BF16)
+    for p in range(3):
+        t = 3 * zl + p if p < 2 else 5 - 3 * zl
+        W[t, y, c, zh, x] = packed[:, 128 * p : 128 * p + 128]
     meet(x, y, z, c)
     copies = Copies(send, recv)
     start, arrive = copies.start, copies.arrive
@@ -114,18 +118,27 @@
     def at(dx=0, dy=0, dz=0):
         return device((x + dx) % 4, (y + dy) % 4, (z + dz) % 8, c)
 
-    def shard(dz):
+    def shard(part, dz):
         zz = (z + dz) % 8
-        return W.at[:, zz % 2, y, c, zz // 2, x]
-
-    def col(part, dx, dy):
-        parts = pl.ds(0, 2) if part == 0 else pl.ds(2, 1)
-        return W.at[parts, :, (y + dy) % 4, c, :, (x + dx) % 4]
+        t = pl.ds(3 * (zz % 2), 2) if part == 0 else pl.ds(5 - 3 * (zz % 2), 1)
+        return W.at[t, y, c, zz // 2, x]
+
+    def col(part, dx, dy, core=c):
+        t = pl.ds(0, 5) if part == 0 else pl.ds(5, 1)
+        return W.at[t, (y + dy) % 4, core, :, (x + dx) % 4]
 
     def half_col(part, dx, dy, half):
         if part == 0:
-            return W.at[half, :, (y + dy) % 4, c, :, (x + dx) % 4]
-        return W.at[2, half, (y + dy) % 4, c, :, (x + dx) % 4]
+            cut = 3 if dy in (0, 1) else 2
+            t = pl.ds(0, cut) if half == 0 else pl.ds(cut, 5 - cut)
+            return W.at[t, (y + dy) % 4, c, :, (x + dx) % 4]
+        return W.at[5, (y + dy) % 4, c, pl.ds(2 * half, 2), (x + dx) % 4]
+
+    def mid_half(part, at_d, d):
+        zhs = pl.ds(0, 2) if d == 1 else pl.ds(2, 2)
+        if part == 0:
+            return W.at[pl.ds(0, 5), (y + at_d) % 4, c, zhs, x]
+        return W.at[5, y, c, zhs, (x + at_d) % 4]
 
     def head(dzl, dy, half):
         rows = slice(None) if half is None else pl.ds(half * 768, 768)
@@ -136,31 +149,39 @@
         start(col(0, 0, d), at(dx=-1), ("p3", 0, 3, d % 4))
         start(col(1, d, 0), at(dy=1), ("p3", 1, 1, d % 4))
         start(col(1, d, 0), at(dy=-1), ("p3", 1, 3, d % 4))
-        start(col(0, 0, d), sib, ("s", 0, 0, d % 4))
-        start(col(1, d, 0), sib, ("s", 1, 0, d % 4))
+        copies.group(col(0, 0, d), sib, ("s",))
+        copies.group(col(1, d, 0), sib, ("s",))
 
     def second_hop(q):
         for d in (1, -1):
             half = 0 if d == 1 else 1
             arrive(col(0, -d, q), sib, ("p3", 0, d % 4, q % 4))
             start(half_col(0, -d, q, half), at(dx=d), ("p4", 0, d % 4, q % 4))
-            start(col(0, -d, q), sib, ("s", 0, d % 4, q % 4))
+            copies.group(col(0, -d, q), sib, ("s",))
             arrive(col(1, q, -d), sib, ("p3", 1, d % 4, q % 4))
             start(half_col(1, q, -d, half), at(dy=d), ("p4", 1, d % 4, q % 4))
-            start(col(1, q, -d), sib, ("s", 1, d % 4, q % 4))
+            copies.group(col(1, q, -d), sib, ("s",))
 
     def last_hop(q):
         for half, d in ((0, 1), (1, -1)):
             arrive(half_col(0, 2, q, half), sib, ("p4", 0, d % 4, q % 4))
             arrive(half_col(1, q, 2, half), sib, ("p4", 1, d % 4, q % 4))
-        start(col(0, 2, q), sib, ("s", 0, 2, q % 4))
-        start(col(1, q, 2), sib, ("s", 1, 2, q % 4))
+        copies.group(col(0, 2, q), sib, ("s",))
+        copies.group(col(1, q, 2), sib, ("s",))
+
+    def head_own(first):
+        for d, half in ((1, 0), (-1, 1)):
+            half = half if first else 1 - half
+            start(head(0, 0, half), at(dy=d), ("hy", d % 4, half))
 
     def head_first():
         for d, half in ((1, 0), (-1, 1)):
             arrive(head(0, -d, half), sib, ("hy", d % 4, half))
+            start(head(0, -d, half), at(dz=d), ("hz", d % 8, -d % 4))
+
+    def head_on():
+        for d, half in ((1, 0), (-1, 1)):
             start(head(0, -d, half), at(dy=d), ("hy2", d % 4))
-            start(head(0, -d, half), at(dz=d), ("hz", d % 8, -d % 4))
 
     def head_second():
         for d, half in ((1, 0), (-1, 1)):
@@ -170,8 +191,8 @@
 
     def head_third():
         arrive(head(0, 2, 0), sib, ("hy2", 1))
+        start(head(0, 2, 0), at(dz=1), ("hz", 1, 2))
         arrive(head(0, 2, 1), sib, ("hy2", 3))
-        start(head(0, 2, 0), at(dz=1), ("hz", 1, 2))
         start(head(0, 2, 1), at(dz=-1), ("hz", 7, 2))
         start(head(0, 2, None), sib, ("hs", 0, 2))
 
@@ -181,42 +202,43 @@
         start(head(1, dy, None), sib, ("hs", 1, dy % 4))
 
     def from_sib():
-        for q in (0, -1, 1, 2):
-            for d in (0, 1, -1, 2):
-                arrive(W.at[pl.ds(0, 2), :, (y + q) % 4, 1 - c, :, (x - d) % 4], sib, ("s", 0, d % 4, q % 4))
-                arrive(W.at[pl.ds(2, 1), :, (y - d) % 4, 1 - c, :, (x + q) % 4], sib, ("s", 1, d % 4, q % 4))
-
-    own[0].wait()
+        arrive(W.at[:, :, 1 - c], sib, ("s",))
+
     for dz in (1, -1, 2, -2, 3, -3, 4):
-        start(shard(0), at(dz=dz), ("z", dz % 8))
-    own[1].wait()
-    for half in (0, 1):
-        start(head(0, 0, half), at(dy=1), ("hy", 1, half))
-        start(head(0, 0, 1 - half), at(dy=-1), ("hy", 3, 1 - half))
+        start(shard(0, 0), at(dz=dz), ("z", 0, dz % 8))
+        start(shard(1, 0), at(dz=dz), ("z", 1, dz % 8))
+    own.wait()
+    head_own(True)
     start(head(0, 0, None), sib, ("hs", 0, 0))
 
     @rows_loop(BINS, 16)
     def _(r):
         v = in_ref[pl.ds(r, 16), :].astype(F32)
         mean_sq = jnp.mean(v * v, axis=-1, keepdims=True)
-        a = gelu(v * lax.rsqrt(mean_sq + 1e-06) * gain_ref[...])
+        a = gelu(v * lax.rsqrt(mean_sq + 1e-06) * gain_ref[...].reshape(1, CH))
         act[pl.ds(r + 8, 16), :] = a.astype(BF16).astype(F32)
 
     start(act.at[pl.ds(8, 8)], before, ("halo", 0), dst=act.at[pl.ds(136, 8)])
     start(act.at[pl.ds(128, 8)], after, ("halo", 1), dst=act.at[pl.ds(0, 8)])
 
     for dz in (1, -1, 2, -2, 3, -3, 4):
-        arrive(shard(-dz), sib, ("z", dz % 8))
-    for d in (1, -1, 2):
+        arrive(shard(0, -dz), sib, ("z", 0, dz % 8))
+        arrive(shard(1, -dz), sib, ("z", 1, dz % 8))
+    for d in (1, -1):
         start(col(0, 0, 0), at(dy=d), ("p2", 0, d % 4))
         start(col(1, 0, 0), at(dx=d), ("p2", 1, d % 4))
     spread(0)
     start(head(0, 0, 0), at(dz=1), ("hz", 1, 0))
     start(head(0, 0, 1), at(dz=-1), ("hz", 7, 0))
+    head_first()
     for d in (1, -1):
         arrive(col(0, 0, -d), sib, ("p2", 0, d % 4))
+        start(mid_half(0, -d, d), at(dy=d), ("p2r", 0, d % 4))
         arrive(col(1, -d, 0), sib, ("p2", 1, d % 4))
+        start(mid_half(1, -d, d), at(dx=d), ("p2r", 1, d % 4))
         spread(-d)
+    second_hop(0)
+    head_own(False)
     arrive(act.at[pl.ds(136, 8)], sib, ("halo", 0))
     arrive(act.at[pl.ds(0, 8)], sib, ("halo", 1))
 
@@ -228,10 +250,11 @@
     def _():
         act[136:144, :] = jnp.zeros((8, CH), F32)
 
-    arrive(col(0, 0, 2), sib, ("p2", 0, 2))
-    arrive(col(1, 2, 0), sib, ("p2", 1, 2))
+    for d in (1, -1):
+        arrive(mid_half(0, 2, d), sib, ("p2r", 0, d % 4))
+        arrive(mid_half(1, 2, d), sib, ("p2r", 1, d % 4))
     spread(2)
-    head_first()
+    head_on()
 
     @rows_loop(BINS, 16)
     def _(r):
@@ -243,18 +266,20 @@
                 AP[g % 2, g // 2, pl.ds(r, 16), :] = jnp.concatenate(pieces, axis=1).astype(BF16)
 
     start(AP.at[1 - c], sib, ("ax",), dst=AX)
-    second_hop(0)
+    last_hop(0)
+    head_second()
     second_hop(-1)
-    head_second()
     second_hop(1)
     second_hop(2)
-    for q in (0, -1, 1, 2):
-        last_hop(q)
     head_third()
+    last_hop(-1)
+    last_hop(1)
+    last_hop(2)
     from_sib()
 
     def w(p, j, cc):
-        return W[p, j // 4, j % 4, cc].reshape(INNER, 128)
+        t = 3 * (j // 4) + p if p < 2 else 5 - 3 * (j // 4)
+        return W[t, j % 4, cc].reshape(INNER, 128)
 
     conv[...] = jnp.zeros_like(conv)
 
@@ -286,28 +311,35 @@
 
     dtower[...] = jnp.zeros_like(dtower)
 
-    def head_step(zz, yy, cc):
-        lanes = pl.ds(pl.multiple_of((zz * 8 + yy * 2 + cc) * 256, 256), 256)
-        weight = H[zz, yy, cc]
-        logits = jnp.dot(tower[...], weight, preferred_element_type=F32) + bias_ref[:, lanes]
+    def head_step(zz, yy):
+        lanes = pl.ds(pl.multiple_of((zz * 4 + yy) * 512, 512), 512)
+        weight = jnp.concatenate([H[zz, yy, 0], H[zz, yy, 1]], axis=1)
+        logits = jnp.dot(tower[...], weight, preferred_element_type=F32) + bias_ref[lanes].reshape(1, -1)
         e = jnp.exp(-jnp.abs(logits))
         pred_ref[:, lanes] = (jnp.maximum(logits, 0.0) + jnp.log1p(e)).astype(BF16)
         sigmoid = jnp.where(logits >= 0.0, 1.0, e) / (1.0 + e)
         dlogits = (cot_ref[:, lanes].astype(F32) * sigmoid).astype(BF16)
         dtower[...] += lax.dot_general(dlogits, weight, LAST, preferred_element_type=F32)
 
-    for cc in (0, 1):
-        for dzl in (0, 1):
-            for dy in (0, -1, 1, 2):
-                piece = H.at[(zl + dzl) % 2, (y + dy) % 4, (c + cc) % 2]
-                if cc == 1:
-                    arrive(piece, sib, ("hs", dzl, dy % 4))
-
-    def head_loop(g, carry):
-        head_step(g // 8, (g // 2) % 4, g % 2)
-        return carry
-
-    lax.fori_loop(0, 16, head_loop, 0)
+    def ready(dzl, dy):
+        arrive(H.at[(zl + dzl) % 2, (y + dy) % 4, 1 - c], sib, ("hs", dzl, dy % 4))
+
+    for dy in (0, -1, 1, 2):
+        ready(0, dy)
+
+    def head_loop(dzl):
+        def one(j, carry):
+            head_step((zl + dzl) % 2, j)
+            return carry
+
+        lax.fori_loop(0, 4, one, 0)
+
+    head_loop(0)
+    for dy in (0, -1, 1, 2):
+        ready(1, dy)
+    head_loop(1)
+    out = pltpu.make_async_copy(pred_ref, pred_out, local.at[1])
+    out.start()
 
     @rows_loop(BINS, 16)
     def _(r):
@@ -391,7 +423,7 @@
         def _(r):
             v = in_ref[pl.ds(r, 16), :].astype(F32)
             rs = lax.rsqrt(jnp.mean(v * v, axis=-1, keepdims=True) + 1e-06)
-            gain = gain_ref[...]
+            gain = gain_ref[...].reshape(1, CH)
             dz = dact[pl.ds(r, 16), :] * gelu_slope(v * rs * gain) * gain
             dot = jnp.mean(dz * v, axis=-1, keepdims=True)
             ig = dtower[pl.ds(r, 16), :] + dz * rs - v * (rs * rs * rs * dot)
@@ -521,17 +553,32 @@
         jobs.pop(0)()
     for p in range(3):
         last_receive(p)
+    copies.of(W.at[:, :, c], W.at[:, :, c], sib, ("s",)).wait_send()
     copies.finish()
-    assert len(copies.ids) <= N_COPIES, len(copies.ids)
+    out.wait()
+    assert len(copies.ids) == N_COPIES, len(copies.ids)
+
+
+def finish_kernel(pred_ref, ig_ref, grad_ref, pred_out, ig_out, conv_out, mix_out, sems):
+    jobs = [pltpu.make_async_copy(ig_ref, ig_out, sems.at[4])]
+    for i in range(4):
+        rows = pl.ds(32 * i, 32)
+        jobs.append(pltpu.make_async_copy(pred_ref.at[rows], pred_out.at[rows], sems.at[i]))
+    for job in jobs:
+        job.start()
+    packed = jnp.concatenate([grad_ref[p] for p in range(3)], axis=1)
+    for k in range(3):
+        conv_out[k] = packed[:, 96 * k : 96 * k + 96]
+    mix_out[...] = packed[:, 288:384]
+    for job in jobs:
+        job.wait()
 
 
 def body(tower_input, norm_gain, conv_weight, mix_weight, head_weight, head_bias, pred_cotangent):
-    shard = jnp.concatenate([conv_weight.transpose(2, 0, 1), mix_weight[:, None, :]], axis=1)
-    shard = shard.reshape(48, 3, 128).transpose(1, 0, 2)
     vmem = pl.BlockSpec(memory_space=pltpu.VMEM)
     hbm = pl.BlockSpec(memory_space=pl.ANY)
     scratch = [
-        ((3, 2, 4, 2, 4, 4, 48, 128), BF16),
+        ((6, 4, 2, 4, 4, 48, 128), BF16),
         ((2, 4, 2, CH, 256), BF16),
         ((BINS + 16, CH), F32),
         ((2, 8, BINS, 384), BF16),
@@ -548,6 +595,7 @@
         ((INNER, 256), BF16),
         ((3, BINS, INNER), BF16),
         ((BINS, CH), F32),
+        ((BINS, TRACKS), BF16),
         ((3, 2, 4, 4, 4, 48, 128), BF16),
         ((2, 3, 4, 4, 48, 128), BF16),
         ((2, 3, 4, 4, 48, 128), BF16),
@@ -567,8 +615,8 @@
             jax.ShapeDtypeStruct((BINS, CH), BF16),
             jax.ShapeDtypeStruct((3, 48, 128), F32),
         ],
-        in_specs=[hbm, hbm, vmem, vmem, vmem, vmem],
-        out_specs=[vmem, vmem, vmem],
+        in_specs=[vmem, vmem, hbm, vmem, vmem, vmem, vmem],
+        out_specs=[hbm, vmem, vmem],
         scratch_shapes=[pltpu.VMEM(*spec) for spec in scratch]
         + [
             pltpu.SemaphoreType.DMA((N_COPIES,)),
@@ -580,17 +628,28 @@
         ),
         name="block",
     )(
-        shard,
+        conv_weight.transpose(0, 2, 1),
+        mix_weight,
         head_weight,
         tower_input[0],
-        norm_gain.reshape(1, CH),
-        head_bias.reshape(1, TRACKS),
+        norm_gain,
+        head_bias,
         pred_cotangent[0],
     )
-    grads = grads.transpose(1, 0, 2).reshape(48, 4, 96)
-    conv_grad = grads[:, :3].transpose(1, 2, 0)
-    mix_grad = grads[:, 3]
-    return (predictions[None], input_grad[None], conv_grad, mix_grad)
+    predictions, input_grad, conv_grad, mix_grad = pl.pallas_call(
+        finish_kernel,
+        out_shape=[
+            jax.ShapeDtypeStruct((BINS, TRACKS), BF16),
+            jax.ShapeDtypeStruct((BINS, CH), BF16),
+            jax.ShapeDtypeStruct((3, 48, 96), F32),
+            jax.ShapeDtypeStruct((48, 96), F32),
+        ],
+        in_specs=[vmem, vmem, vmem],
+        out_specs=[hbm, hbm, vmem, vmem],
+        scratch_shapes=[pltpu.SemaphoreType.DMA((5,))],
+        name="unpack",
+    )(predictions, input_grad, grads)
+    return (predictions[None], input_grad[None], conv_grad.transpose(0, 2, 1), mix_grad)
 
 
 def solution(mesh):

time: 133 us -> 114 us (0.86)
  Pallas kernels: 124 us -> 113 us
  local copies, waits for them, and re-layouts: 7.47 us -> 0 us
    pallas_call x1, Pallas kernels: 124 us -> 110 us  [body(): pl.pallas_call(kernel, out_shape=[jax.ShapeDtypeStruct((BINS, TRACKS), BF...]
    unnamed x7 -> x0, local copies, waits for them, and re-layouts: 3.73 us -> none
    pallas_call x0 -> x1, Pallas kernels: none -> 3.12 us  [body(): pl.pallas_call(finish_kernel, out_shape=[jax.ShapeDtypeStruct((BINS, TRAC...]
    reshape x4 -> x0, local copies, waits for them, and re-layouts: 2.15 us -> none  [the longest x1 1.3 us: body(): norm_gain.reshape(1, CH)]
where the time goes in v2:
time: 114 us
  Pallas kernels  113 us (99%)
    pallas_call x1, Pallas kernels, body(): pl.pallas_call(kernel, out_shape=[jax.ShapeDtypeStruct((BINS, TRACKS), BF...  110 us
    pallas_call x1, Pallas kernels, body(): pl.pallas_call(finish_kernel, out_shape=[jax.ShapeDtypeStruct((BINS, TRAC...  3.12 us

profile of v2, /device:TPU:8, one launch (start us, length us, event | category | flops | bytes accessed | tf_op | source)
XLA Modules:
  0.0 114.1 jit_solution(4430301546914369187)
XLA Ops:
  0.6 110.3 %block.1 = (bf16[128,4096]{1,0:T(8,128)(2,1)}, bf16[128,1536]{1,0:T(8,128)(2,1)}, f32[3,48,128]{2,1,0:T(8,128)}) custom-call(bf16[3,48,96]{2,1,0:T(8,128)(2,1)} %bitcast.8, bf16[48,96]{1,0:T(8,128)(2,1)} %mix_ref.1, bf16[1536,256]{1,0:T(8,128)(2,1)} %h_ref.1, bf16[128,1536]{1,0:T(8,128)(2,1)} %bitcast.7, f32[1536]{0:T(1024)} %gain_ref.1, f32[4096]{0:T(1024)} %bias_ref.1, ...), custom_call_target="tpu_custom_call" | custom-call | tf_op jit(solution)/shard_map/block/pallas_call | solution.py:611
  111.0 3.1 %unpack.1 = (bf16[128,4096]{1,0:T(8,128)(2,1)}, bf16[128,1536]{1,0:T(8,128)(2,1)}, f32[3,48,96]{2,1,0:T(8,128)}, f32[48,96]{1,0:T(8,128)}) custom-call(bf16[128,4096]{1,0:T(8,128)(2,1)} %get-tuple-element.11.pred_ref, bf16[128,1536]{1,0:T(8,128)(2,1)} %get-tuple-element.12.ig_ref, f32[3,48,128]{2,1,0:T(8,128)} %get-tuple-element.13.grad_ref), custom_call_target="tpu_custom_call" | custom-call | tf_op jit(solution)/shard_map/unpack/pallas_call | solution.py:639

commit v3 on v2

--- a/solution.py
+++ b/solution.py
@@ -93,10 +93,10 @@
 
 
 def kernel(
-    taps_ref, mix_ref, h_ref, in_ref, gain_ref, bias_ref, cot_ref,
+    taps_ref, mix_ref, h_ref, in_ref, gain_ref, bias_ref, cot_in,
     pred_out, ig_ref, grad_ref,
     W, H, act, AP, AX, conv, hidden, tower, dtower, DT, DX, dext, dext16, hT, dT, dh2, dact,
-    pred_ref, G, RX, RY, RZ, M0, M1, M2, L0, L1, L2, sum0,
+    pred_ref, cot_ref, G, RX, RY, RZ, M0, M1, M2, L0, L1, L2, sum0,
     send, recv, local,
 ):
     x, y, z, c = place()
@@ -106,6 +106,8 @@
     before, after = (b, (s + 15) % 16), (b, (s + 1) % 16)
     own = pltpu.make_async_copy(h_ref, H.at[zl, y, c], local.at[0])
     own.start()
+    cot_copy = pltpu.make_async_copy(cot_in, cot_ref, local.at[2])
+    cot_copy.start()
     packed = [taps_ref[k].astype(F32) for k in range(3)] + [mix_ref[...].astype(F32)]
     packed = jnp.concatenate(packed, axis=1).astype(BF16)
     for p in range(3):
@@ -290,7 +292,7 @@
         return carry
 
     lax.fori_loop(0, 8, conv_step, 0)
-    for dy in (0, -1, 1, 2):
+    for dy in (0, -1, 1):
         head_other(dy)
 
     @rows_loop(BINS, 16)
@@ -310,6 +312,7 @@
         tower[:, lanes] = (in_ref[:, lanes].astype(F32) + jnp.concatenate(mixed, axis=1)).astype(BF16)
 
     dtower[...] = jnp.zeros_like(dtower)
+    cot_copy.wait()
 
     def head_step(zz, yy):
         lanes = pl.ds(pl.multiple_of((zz * 4 + yy) * 512, 512), 512)
@@ -324,20 +327,12 @@
     def ready(dzl, dy):
         arrive(H.at[(zl + dzl) % 2, (y + dy) % 4, 1 - c], sib, ("hs", dzl, dy % 4))
 
-    for dy in (0, -1, 1, 2):
-        ready(0, dy)
-
-    def head_loop(dzl):
-        def one(j, carry):
-            head_step((zl + dzl) % 2, j)
-            return carry
-
-        lax.fori_loop(0, 4, one, 0)
-
-    head_loop(0)
-    for dy in (0, -1, 1, 2):
-        ready(1, dy)
-    head_loop(1)
+    for dzl in (0, 1):
+        for dy in (0, -1, 1, 2):
+            ready(dzl, dy)
+            head_step((zl + dzl) % 2, (y + dy) % 4)
+            if dzl == 0 and dy == -1:
+                head_other(2)
     out = pltpu.make_async_copy(pred_ref, pred_out, local.at[1])
     out.start()
 
@@ -373,12 +368,12 @@
     start(dext.at[pl.ds(128, 8)], after, ("dhalo", 1), dst=dext.at[pl.ds(0, 8)])
 
     arrive(dh2.at[0], sib, ("hidden",))
-    arrive(dh2.at[1], sib, ("dconv",))
-    arrive(AX, sib, ("ax",))
-    arrive(DX, sib, ("dt",))
     hT[:, 0:128] = hidden[...].T
     hT[:, 128:256] = dh2[0].T
     dT[:, 0:128] = dh2[2].T
+    arrive(AX, sib, ("ax",))
+    arrive(DX, sib, ("dt",))
+    arrive(dh2.at[1], sib, ("dconv",))
     dT[:, 128:256] = dh2[1].T
 
     def grad_step(j, carry):
@@ -559,19 +554,16 @@
     assert len(copies.ids) == N_COPIES, len(copies.ids)
 
 
-def finish_kernel(pred_ref, ig_ref, grad_ref, pred_out, ig_out, conv_out, mix_out, sems):
-    jobs = [pltpu.make_async_copy(ig_ref, ig_out, sems.at[4])]
-    for i in range(4):
-        rows = pl.ds(32 * i, 32)
-        jobs.append(pltpu.make_async_copy(pred_ref.at[rows], pred_out.at[rows], sems.at[i]))
-    for job in jobs:
-        job.start()
-    packed = jnp.concatenate([grad_ref[p] for p in range(3)], axis=1)
-    for k in range(3):
-        conv_out[k] = packed[:, 96 * k : 96 * k + 96]
-    mix_out[...] = packed[:, 288:384]
-    for job in jobs:
-        job.wait()
+def finish_kernel(pred_ref, ig_ref, grad_ref, pred_out, ig_out, conv_out, mix_out):
+    pred_out[...] = pred_ref[...]
+    ig_out[...] = ig_ref[...]
+
+    @pl.when(pl.program_id(0) == 0)
+    def _():
+        packed = jnp.concatenate([grad_ref[p] for p in range(3)], axis=1)
+        for k in range(3):
+            conv_out[k] = packed[:, 96 * k : 96 * k + 96]
+        mix_out[...] = packed[:, 288:384]
 
 
 def body(tower_input, norm_gain, conv_weight, mix_weight, head_weight, head_bias, pred_cotangent):
@@ -596,6 +588,7 @@
         ((3, BINS, INNER), BF16),
         ((BINS, CH), F32),
         ((BINS, TRACKS), BF16),
+        ((BINS, TRACKS), BF16),
         ((3, 2, 4, 4, 4, 48, 128), BF16),
         ((2, 3, 4, 4, 48, 128), BF16),
         ((2, 3, 4, 4, 48, 128), BF16),
@@ -615,13 +608,13 @@
             jax.ShapeDtypeStruct((BINS, CH), BF16),
             jax.ShapeDtypeStruct((3, 48, 128), F32),
         ],
-        in_specs=[vmem, vmem, hbm, vmem, vmem, vmem, vmem],
+        in_specs=[vmem, vmem, hbm, vmem, vmem, vmem, hbm],
         out_specs=[hbm, vmem, vmem],
         scratch_shapes=[pltpu.VMEM(*spec) for spec in scratch]
         + [
             pltpu.SemaphoreType.DMA((N_COPIES,)),
             pltpu.SemaphoreType.DMA((N_COPIES,)),
-            pltpu.SemaphoreType.DMA((2,)),
+            pltpu.SemaphoreType.DMA((3,)),
         ],
         compiler_params=pltpu.CompilerParams(
             collective_id=0, has_side_effects=True, vmem_limit_bytes=60 * 2**20
@@ -644,9 +637,18 @@
             jax.ShapeDtypeStruct((3, 48, 96), F32),
             jax.ShapeDtypeStruct((48, 96), F32),
         ],
-        in_specs=[vmem, vmem, vmem],
-        out_specs=[hbm, hbm, vmem, vmem],
-        scratch_shapes=[pltpu.SemaphoreType.DMA((5,))],
+        grid=(4,),
+        in_specs=[
+            pl.BlockSpec((32, TRACKS), lambda i: (i, 0)),
+            pl.BlockSpec((32, CH), lambda i: (i, 0)),
+            pl.BlockSpec((3, 48, 128), lambda i: (0, 0, 0)),
+        ],
+        out_specs=[
+            pl.BlockSpec((32, TRACKS), lambda i: (i, 0)),
+            pl.BlockSpec((32, CH), lambda i: (i, 0)),
+            pl.BlockSpec((3, 48, 96), lambda i: (0, 0, 0)),
+            pl.BlockSpec((48, 96), lambda i: (0, 0)),
+        ],
         name="unpack",
     )(predictions, input_grad, grads)
     return (predictions[None], input_grad[None], conv_grad.transpose(0, 2, 1), mix_grad)

time: 114 us -> 112 us (0.982)
  Pallas kernels: 113 us -> 111 us
    pallas_call x1, Pallas kernels: 110 us -> 107 us  [body(): pl.pallas_call(kernel, out_shape=[jax.ShapeDtypeStruct((BINS, TRACKS), BF...]
where the time goes in v3:
time: 112 us
  Pallas kernels  111 us (99%)
    pallas_call x1, Pallas kernels, body(): pl.pallas_call(kernel, out_shape=[jax.ShapeDtypeStruct((BINS, TRACKS), BF...  107 us
    pallas_call x1, Pallas kernels, body(): pl.pallas_call(finish_kernel, out_shape=[jax.ShapeDtypeStruct((BINS, TRAC...  3.66 us

profile of v3, /device:TPU:8, one launch (start us, length us, event | category | flops | bytes accessed | tf_op | source)
XLA Modules:
  0.0 111.7 jit_solution(3907887959294170760)
XLA Ops:
  0.6 107.2 %block.1 = (bf16[128,4096]{1,0:T(8,128)(2,1)}, bf16[128,1536]{1,0:T(8,128)(2,1)}, f32[3,48,128]{2,1,0:T(8,128)}) custom-call(bf16[3,48,96]{2,1,0:T(8,128)(2,1)} %bitcast.8, bf16[48,96]{1,0:T(8,128)(2,1)} %mix_ref.1, bf16[1536,256]{1,0:T(8,128)(2,1)} %h_ref.1, bf16[128,1536]{1,0:T(8,128)(2,1)} %bitcast.7, f32[1536]{0:T(1024)} %gain_ref.1, f32[4096]{0:T(1024)} %bias_ref.1, ...), custom_call_target="tpu_custom_call" | custom-call | tf_op jit(solution)/shard_map/block/pallas_call | solution.py:604
  107.8 3.7 %unpack.1 = (bf16[128,4096]{1,0:T(8,128)(2,1)}, bf16[128,1536]{1,0:T(8,128)(2,1)}, f32[3,48,96]{2,1,0:T(8,128)}, f32[48,96]{1,0:T(8,128)}) custom-call(bf16[128,4096]{1,0:T(8,128)(2,1)} %get-tuple-element.11.pred_ref, bf16[128,1536]{1,0:T(8,128)(2,1)} %get-tuple-element.12.ig_ref, f32[3,48,128]{2,1,0:T(8,128)} %get-tuple-element.13.grad_ref), custom_call_target="tpu_custom_call" | custom-call | tf_op jit(solution)/shard_map/unpack/pallas_call | solution.py:632

commit v4 on v3

--- a/solution.py
+++ b/solution.py
@@ -286,12 +286,13 @@
     conv[...] = jnp.zeros_like(conv)
 
     def conv_step(j, carry):
-        lhs = jnp.concatenate([AP[0, j], AP[1, j]], axis=1)
-        rhs = jnp.concatenate([w(p, j, cc) for cc in range(2) for p in range(3)], axis=1)
+        two = [(2 * j + i, cc) for i in range(2) for cc in range(2)]
+        lhs = jnp.concatenate([AP[cc, i] for i, cc in two], axis=1)
+        rhs = jnp.concatenate([w(p, i, cc) for i, cc in two for p in range(3)], axis=1)
         conv[...] += lax.dot_general(lhs, rhs, LAST, preferred_element_type=F32)
         return carry
 
-    lax.fori_loop(0, 8, conv_step, 0)
+    lax.fori_loop(0, 4, conv_step, 0)
     for dy in (0, -1, 1):
         head_other(dy)
 
@@ -349,12 +350,13 @@
     sum0[...] = jnp.zeros_like(sum0)
 
     def dhidden_step(j, carry):
-        lhs = jnp.concatenate([DT[0, j], DT[1, j]], axis=1)
-        rhs = jnp.concatenate([w(2, j, 0), w(2, j, 1)], axis=1)
+        four = [(4 * j + i, cc) for i in range(4) for cc in range(2)]
+        lhs = jnp.concatenate([DT[cc, i] for i, cc in four], axis=1)
+        rhs = jnp.concatenate([w(2, i, cc) for i, cc in four], axis=1)
         sum0[...] += lax.dot_general(lhs, rhs, LAST, preferred_element_type=F32)
         return carry
 
-    lax.fori_loop(0, 8, dhidden_step, 0)
+    lax.fori_loop(0, 2, dhidden_step, 0)
 
     @rows_loop(BINS, 16)
     def _(r):
@@ -376,18 +378,21 @@
     arrive(dh2.at[1], sib, ("dconv",))
     dT[:, 128:256] = dh2[1].T
 
-    def grad_step(j, carry):
-        rhs = jnp.concatenate([AP[c, j], AX[j]], axis=0)
-        g = jnp.dot(dT[...], rhs, preferred_element_type=F32)
-        more = jnp.dot(hT[...], jnp.concatenate([DT[c, j], DX[j]], axis=0), preferred_element_type=F32)
-        for p in range(3):
-            part = g[:, 128 * p : 128 * p + 128]
-            if p == 2:
-                part = part + more
-            G[p, j // 4, j % 4] = part.astype(BF16).reshape(4, 4, 48, 128)
+    def grad_step(i, carry):
+        two = (2 * i, 2 * i + 1)
+        rhs = [jnp.concatenate([AP[c, j], AX[j]], axis=0) for j in two]
+        g = jnp.dot(dT[...], jnp.concatenate(rhs, axis=1), preferred_element_type=F32)
+        rhs = [jnp.concatenate([DT[c, j], DX[j]], axis=0) for j in two]
+        more = jnp.dot(hT[...], jnp.concatenate(rhs, axis=1), preferred_element_type=F32)
+        for n, j in enumerate(two):
+            for p in range(3):
+                part = g[:, 384 * n + 128 * p : 384 * n + 128 * p + 128]
+                if p == 2:
+                    part = part + more[:, 128 * n : 128 * n + 128]
+                G[p, j // 4, j % 4] = part.astype(BF16).reshape(4, 4, 48, 128)
         return carry
 
-    lax.fori_loop(0, 8, grad_step, 0)
+    lax.fori_loop(0, 4, grad_step, 0)
 
     def dact_prepare():
         arrive(dext.at[pl.ds(136, 8)], sib, ("dhalo", 0))

time: 112 us -> 109 us (0.973)
  Pallas kernels: 111 us -> 108 us
    pallas_call x1, Pallas kernels: 107 us -> 104 us  [body(): pl.pallas_call(kernel, out_shape=[jax.ShapeDtypeStruct((BINS, TRACKS), BF...]
where the time goes in v4:
time: 109 us
  Pallas kernels  108 us (99%)
    pallas_call x1, Pallas kernels, body(): pl.pallas_call(kernel, out_shape=[jax.ShapeDtypeStruct((BINS, TRACKS), BF...  104 us
    pallas_call x1, Pallas kernels, body(): pl.pallas_call(finish_kernel, out_shape=[jax.ShapeDtypeStruct((BINS, TRAC...  3.66 us

profile of v4, /device:TPU:8, one launch (start us, length us, event | category | flops | bytes accessed | tf_op | source)
XLA Modules:
  0.0 108.6 jit_solution(7832757766906677872)
XLA Ops:
  0.6 104.2 %block.1 = (bf16[128,4096]{1,0:T(8,128)(2,1)}, bf16[128,1536]{1,0:T(8,128)(2,1)}, f32[3,48,128]{2,1,0:T(8,128)}) custom-call(bf16[3,48,96]{2,1,0:T(8,128)(2,1)} %bitcast.8, bf16[48,96]{1,0:T(8,128)(2,1)} %mix_ref.1, bf16[1536,256]{1,0:T(8,128)(2,1)} %h_ref.1, bf16[128,1536]{1,0:T(8,128)(2,1)} %bitcast.7, f32[1536]{0:T(1024)} %gain_ref.1, f32[4096]{0:T(1024)} %bias_ref.1, ...), custom_call_target="tpu_custom_call" | custom-call | tf_op jit(solution)/shard_map/block/pallas_call | solution.py:609
  104.8 3.7 %unpack.1 = (bf16[128,4096]{1,0:T(8,128)(2,1)}, bf16[128,1536]{1,0:T(8,128)(2,1)}, f32[3,48,96]{2,1,0:T(8,128)}, f32[48,96]{1,0:T(8,128)}) custom-call(bf16[128,4096]{1,0:T(8,128)(2,1)} %get-tuple-element.11.pred_ref, bf16[128,1536]{1,0:T(8,128)(2,1)} %get-tuple-element.12.ig_ref, f32[3,48,128]{2,1,0:T(8,128)} %get-tuple-element.13.grad_ref), custom_call_target="tpu_custom_call" | custom-call | tf_op jit(solution)/shard_map/unpack/pallas_call | solution.py:637
